TPU v7x, 32 devices: a whole 2x2x4 slice. The times are simulated.
32 devices in a mesh: patch: 4 (over y, core), map: 8 (over z, x).
Axes of the slice: x: 2, y: 2, z: 4, core: 2. Of those that a mesh axis runs over, the one named last changes fastest.
Arguments:
- maps: bfloat16 [16, 32, 6144], P('map', None, 'patch'), may hold values from -6 to 6
- cotangent: bfloat16 [16, 32, 6144], P('map', None, 'patch'), may hold values from -6 to 6
- tiles: bfloat16 [24, 3, 256, 256], P('patch'), may hold values from -0.21875 to 0.21875
- columns: int32 [24, 3], P('patch'), may hold values from 0 to 23, as said below
- filters: bfloat16 [3, 32, 32], replicated, may hold values from -0.625 to 0.625
Outputs:
- output: bfloat16 [16, 32, 6144], P('map', None, 'patch')
- input_grad: bfloat16 [16, 32, 6144], P('map', None, 'patch')
- filter_grad: float32 [3, 32, 32], replicated
Inputs may be any that keep to these rules, and one draw needn't show every extreme that they name: `columns`: slot 0 of block row b names block b itself, slot 1 a block 1 to 2 before it and slot 2 a block 1 to 2 after it, counted cyclically over the 24 blocks; block row 0 reads exactly 2 blocks away on both sides.
All inputs are finite; a program needn't handle non-finite values.
Results may differ from a plain program's by a relative error of at most 0.0054.
Values may be sent and summed in bfloat16 or wider, within the bound.
A program may use at most 64 MiB of HBM per device.

v0:
```python
import functools
import math

import jax
import jax.numpy as jnp
from jax import lax
from jax.experimental import pallas as pl
from jax.experimental.pallas import tpu as pltpu
from jax.sharding import PartitionSpec as P

REACH = 2
MESH = pl.DeviceIdType.MESH
F32 = jnp.float32
BF16 = jnp.bfloat16


def dot_nn(a, b):
    return lax.dot_general(a, b, (((1,), (0,)), ((), ())), preferred_element_type=F32)


def dot_nt(a, b):
    return lax.dot_general(a, b, (((1,), (1,)), ((), ())), preferred_element_type=F32)


def mixing(filters, copies):
    order, chan = filters.shape[0], filters.shape[1]
    zero = jnp.zeros((chan, chan), F32)
    adjoint, output = [], []
    for m in range(copies):
        adjoint.append([])
        output.append([])
        for k in list(range(order)) + [order - 1]:
            term = filters[k].astype(F32)
            for n in range(copies):
                adjoint[m].append(term if n == m else zero)
                output[m].append(term.T if n == m else zero)
    join = lambda rows: jnp.concatenate([jnp.concatenate(r, axis=1) for r in rows], axis=0).astype(BF16)
    return join(adjoint), join(output)


def kernel(
    patch_count,
    map_count,
    copies,
    scale,
    maps,
    cot,
    tiles_hbm,
    cols_hbm,
    filters_hbm,
    out,
    grad,
    filter_grad,
    cols,
    filters,
    tiles,
    turned_tiles,
    x_zero,
    x_one,
    y_zero,
    y_one,
    acc_x,
    acc_y,
    to_left,
    to_right,
    from_left,
    from_right,
    early_patch,
    early_map,
    late_patch,
    late_map,
    mix_out,
    mix_in,
    load_cols,
    load_filters,
    load_tile,
    load_x,
    load_y,
    halo_send,
    halo_recv,
    adj_send,
    adj_recv,
    patch_send,
    patch_recv,
    map_send,
    map_recv,
):
    nb, _, bs, _ = tiles.shape
    reach = REACH
    me, my_map = lax.axis_index("patch"), lax.axis_index("map")
    left = lax.rem(me + patch_count - 1, patch_count)
    right = lax.rem(me + 1, patch_count)
    total = patch_count * nb
    low = list(range(reach))
    high = list(range(nb - reach, nb))
    middle = list(range(reach, nb - reach))
    edges = [b for pair in zip(low, reversed(high)) for b in pair]
    order = edges + middle

    barrier = pltpu.get_barrier_semaphore()
    for d in range(1, patch_count):
        pl.semaphore_signal(barrier, inc=1, device_id=(lax.rem(me + d, patch_count), my_map), device_id_type=MESH)
    for d in range(1, map_count):
        pl.semaphore_signal(barrier, inc=1, device_id=(me, lax.rem(my_map + d, map_count)), device_id_type=MESH)

    loads_y = [pltpu.make_async_copy(cot.at[:, pl.ds(b * bs, bs)], y_zero.at[b], load_y.at[b]) for b in range(nb)]
    loads_x = [pltpu.make_async_copy(maps.at[:, pl.ds(b * bs, bs)], x_zero.at[reach + b], load_x.at[b]) for b in range(nb)]
    loads_t = [pltpu.make_async_copy(tiles_hbm.at[b], tiles.at[b], load_tile.at[b]) for b in range(nb)]
    load_f = pltpu.make_async_copy(filters_hbm, filters, load_filters)
    load_f.start()
    load_c = pltpu.make_async_copy(cols_hbm, cols, load_cols)
    load_c.start()
    for b in order:
        loads_y[b].start()
        loads_t[b].start()
    for b in order:
        loads_x[b].start()

    def remote(src, dst, send_sem, recv_sem, patch, map_index):
        copy = pltpu.make_async_remote_copy(
            src_ref=src,
            dst_ref=dst,
            send_sem=send_sem,
            recv_sem=recv_sem,
            device_id=(patch, map_index),
            device_id_type=MESH,
        )
        copy.start()
        return copy

    sent = []

    def send_maps():
        copies_ = []
        for i in range(reach):
            copies_.append(
                remote(
                    maps.at[:, pl.ds(i * bs, bs)],
                    x_zero.at[reach + nb + i],
                    halo_send.at[0, 0, i],
                    halo_recv.at[0, 0, i],
                    left,
                    my_map,
                )
            )
            copies_.append(
                remote(
                    maps.at[:, pl.ds((nb - reach + i) * bs, bs)],
                    x_zero.at[i],
                    halo_send.at[0, 1, i],
                    halo_recv.at[0, 1, i],
                    right,
                    my_map,
                )
            )
        sent.extend(copies_)
        return copies_

    def send_x_one():
        copies_ = [
            remote(
                x_one.at[pl.ds(reach, reach)],
                x_one.at[pl.ds(reach + nb, reach)],
                halo_send.at[1, 0, 0],
                halo_recv.at[1, 0, 0],
                left,
                my_map,
            ),
            remote(
                x_one.at[pl.ds(nb, reach)],
                x_one.at[pl.ds(0, reach)],
                halo_send.at[1, 1, 0],
                halo_recv.at[1, 1, 0],
                right,
                my_map,
            ),
        ]
        sent.extend(copies_)
        return copies_

    chan = filters.shape[1]
    half = copies * chan
    width = 2 * half

    def fold(value):
        result = value[:chan]
        for m in range(1, copies):
            result = result + pltpu.roll(value[m * chan : (m + 1) * chan], width - m * chan, 1)
        return result

    def lanes(parts):
        lane = lax.broadcasted_iota(jnp.int32, parts[0].shape, 1)
        return jnp.where(
            lane < chan,
            parts[0],
            jnp.where(
                lane < half,
                pltpu.roll(parts[1], chan, 1),
                jnp.where(lane < half + chan, parts[2], pltpu.roll(parts[3], chan, 1)),
            ),
        )

    def start_patch(stage, buffer, value):
        buffer[me] = value
        copies_ = [
            remote(
                buffer.at[me],
                buffer.at[me],
                patch_send.at[stage, d - 1],
                patch_recv.at[stage, d - 1],
                lax.rem(me + d, patch_count),
                my_map,
            )
            for d in range(1, patch_count)
        ]
        sent.extend(copies_)
        return copies_

    def total_of(buffer, count, copies_):
        for copy in copies_:
            copy.wait_recv()
        result = buffer[0]
        for i in range(1, count):
            result = result + buffer[i]
        return result

    def start_map(stage, buffer, value):
        buffer[my_map] = value
        copies_ = [
            remote(
                buffer.at[my_map],
                buffer.at[my_map],
                map_send.at[stage, d - 1],
                map_recv.at[stage, d - 1],
                me,
                lax.rem(my_map + d, map_count),
            )
            for d in range(1, map_count)
        ]
        sent.extend(copies_)
        return copies_

    def pick(flag, yes, no):
        return jnp.where(flag, yes, no)

    def keep(flag, value):
        return jnp.where(flag, value, jnp.zeros_like(value))

    def left_part(w, b):
        return dot_nn(w[b], tiles[b, 1])

    def right_part(w, b):
        return dot_nn(w[b], tiles[b, 2])

    def send_adjoint(turn, w):
        p1 = {b: left_part(w, b) for b in low}
        p2 = {b: right_part(w, b) for b in high}
        last = nb - 1
        to_left[turn, 1] = (keep(near_left[0], p1[0]) + keep(~near_left[1], p1[1])).astype(BF16)
        to_left[turn, 0] = keep(~near_left[0], p1[0]).astype(BF16)
        to_right[turn, 0] = (keep(near_right[last], p2[last]) + keep(~near_right[last - 1], p2[last - 1])).astype(BF16)
        to_right[turn, 1] = keep(~near_right[last], p2[last]).astype(BF16)
        copies_ = [
            remote(to_left.at[turn], from_right.at[turn], adj_send.at[turn, 0], adj_recv.at[turn, 0], left, my_map),
            remote(to_right.at[turn], from_left.at[turn], adj_send.at[turn, 1], adj_recv.at[turn, 1], right, my_map),
        ]
        sent.extend(copies_)
        return copies_, p1, p2

    def local_adjoint(w, p1, p2):
        p1, p2 = dict(p1), dict(p2)
        for b in range(nb):
            if b not in p1:
                p1[b] = left_part(w, b)
            if b not in p2:
                p2[b] = right_part(w, b)
        for t in range(nb):
            value = dot_nn(w[t], tiles[t, 0])
            if t + 1 < nb:
                value = value + keep(near_left[t + 1], p1[t + 1])
            if t + 2 < nb:
                value = value + keep(~near_left[t + 2], p1[t + 2])
            if t >= 1:
                value = value + keep(near_right[t - 1], p2[t - 1])
            if t >= 2:
                value = value + keep(~near_right[t - 2], p2[t - 2])
            acc_y[t] = value

    def whole_adjoint(turn, t):
        value = acc_y[t]
        if t < reach:
            value = value + from_left[turn, t].astype(F32)
        if t >= nb - reach:
            value = value + from_right[turn, t - (nb - reach)].astype(F32)
        return value

    def turned(field, b, slot):
        if field is x_zero:
            turned_tiles[b, slot] = tiles[b, slot].T
        return turned_tiles[b, slot]

    def own_term(field, b):
        return dot_nn(field[reach + b], turned(field, b, 0))

    def left_term(field, b):
        return dot_nn(pick(near_left[b], field[reach + b - 1], field[reach + b - 2]), turned(field, b, 1))

    def right_term(field, b):
        return dot_nn(pick(near_right[b], field[reach + b + 1], field[reach + b + 2]), turned(field, b, 2))

    def inner_forward(field, b):
        value = own_term(field, b)
        if b >= reach:
            value = value + left_term(field, b)
        if b < nb - reach:
            value = value + right_term(field, b)
        return value

    def rest_forward(field, b):
        return left_term(field, b) if b < reach else right_term(field, b)

    pl.semaphore_wait(barrier, patch_count + map_count - 2)
    halo = send_maps()
    load_c.wait()
    near_left = [lax.rem(me * nb + b - cols[1, b] + total, total) == 1 for b in range(nb)]
    near_right = [lax.rem(cols[2, b] - me * nb - b + total, total) == 1 for b in range(nb)]
    for b in edges:
        loads_y[b].wait()
        loads_t[b].wait()
    adj, p1, p2 = send_adjoint(0, y_zero)
    load_f.wait()
    mix_in[...], mix_out[...] = mixing(filters, copies)
    for b in middle:
        loads_y[b].wait()
        loads_t[b].wait()
    for b in range(nb):
        loads_x[b].wait()
    for b in edges:
        acc_x[b] = inner_forward(x_zero, b)
    for b in middle:
        x_one[reach + b] = inner_forward(x_zero, b).astype(BF16)
    for copy in halo:
        copy.wait_recv()
    for b in edges:
        x_one[reach + b] = (acc_x[b] + rest_forward(x_zero, b)).astype(BF16)
    halo = send_x_one()

    product = None
    for b in range(nb):
        rows = jnp.concatenate([x_zero[reach + b], x_one[reach + b]], axis=0)
        term = dot_nt(rows, jnp.concatenate([y_zero[b], y_zero[b]], axis=0))
        product = term if product is None else product + term
    zeroth, first_order = fold(product[:half]), fold(product[half:])
    mid = chan // 2
    early = start_patch(0, early_patch, lanes([zeroth[:mid], zeroth[mid:], first_order[:mid], first_order[mid:]]))

    local_adjoint(y_zero, p1, p2)
    for copy in adj:
        copy.wait_recv()
    product = None
    for b in range(nb):
        y_one[b] = whole_adjoint(0, b).astype(BF16)
        term = dot_nt(x_one[reach + b], jnp.concatenate([y_one[b], y_one[b]], axis=0))
        product = term if product is None else product + term
    second = fold(product)
    quarter = chan // 4
    late = start_patch(1, late_patch, lanes([second[i * quarter : (i + 1) * quarter] for i in range(4)]))

    adj, p1, p2 = send_adjoint(1, y_one)
    early = start_map(0, early_map, total_of(early_patch, patch_count, early))
    for b in edges:
        acc_x[b] = inner_forward(x_one, b)

    def write_output(b, applied):
        first = x_zero[reach + b]
        x_two = (2.0 * applied - first.astype(F32)).astype(BF16)
        terms = jnp.concatenate([first, x_one[reach + b], x_two], axis=0)
        out[:, b * bs : (b + 1) * bs] = dot_nn(mix_out[:, : terms.shape[0]], terms).astype(BF16)

    def write_grad(b):
        first = y_zero[b]
        y_two = 2.0 * whole_adjoint(1, b) - first.astype(F32)
        coarse = y_two.astype(BF16)
        fine = (y_two - coarse.astype(F32)).astype(BF16)
        terms = jnp.concatenate([first, y_one[b], coarse, fine], axis=0)
        grad[:, b * bs : (b + 1) * bs] = dot_nn(mix_in[...], terms).astype(BF16)

    late = start_map(1, late_map, total_of(late_patch, patch_count, late))
    local_adjoint(y_one, p1, p2)
    for b in middle:
        write_output(b, inner_forward(x_one, b))
        write_grad(b)
    for copy in halo:
        copy.wait_recv()
    for b in edges:
        write_output(b, acc_x[b] + rest_forward(x_one, b))
    for copy in adj:
        copy.wait_recv()
    for b in edges:
        write_grad(b)
    whole = total_of(early_map, map_count, early) * scale
    shifted = [pltpu.roll(whole, width - i * chan, 1)[:, :chan] if i else whole[:, :chan] for i in range(4)]
    filter_grad[0, :mid], filter_grad[0, mid:] = shifted[0], shifted[1]
    filter_grad[1, :mid], filter_grad[1, mid:] = shifted[2], shifted[3]
    whole = total_of(late_map, map_count, late) * scale
    for i in range(4):
        lines = slice(i * quarter, (i + 1) * quarter)
        part = pltpu.roll(whole, width - i * chan, 1)[:, :chan] if i else whole[:, :chan]
        filter_grad[2, lines] = 2.0 * part - filter_grad[0, lines]
    for copy in sent:
        copy.wait_send()


def write(out, grad, filter_grad, out_hbm, grad_hbm, filter_grad_hbm, sems):
    copies = [
        pltpu.make_async_copy(out, out_hbm, sems.at[0]),
        pltpu.make_async_copy(grad, grad_hbm, sems.at[1]),
        pltpu.make_async_copy(filter_grad, filter_grad_hbm, sems.at[2]),
    ]
    for copy in copies:
        copy.start()
    for copy in copies:
        copy.wait()


def per_device(patch_count, map_count, maps, cotangent, tiles, columns, filters):
    copies, chan, pix = maps.shape
    nb, slots, bs, _ = tiles.shape
    rows = copies * chan
    order = filters.shape[0]
    scale = 1.0 / math.sqrt(copies * map_count * pix * patch_count)
    hbm = pl.BlockSpec(memory_space=pltpu.HBM)
    vmem = pl.BlockSpec(memory_space=pltpu.VMEM)
    dma = pltpu.SemaphoreType.DMA
    field = pltpu.VMEM((nb + 2 * REACH, rows, bs), BF16)
    own = pltpu.VMEM((nb, rows, bs), BF16)
    wide = pltpu.VMEM((nb, rows, bs), F32)
    rim = pltpu.VMEM((2, REACH, rows, bs), BF16)
    pin = lambda x: pltpu.with_memory_space_constraint(x, pltpu.HBM)
    results = (
        jax.ShapeDtypeStruct((rows, pix), BF16),
        jax.ShapeDtypeStruct((rows, pix), BF16),
        jax.ShapeDtypeStruct((order, chan, chan), F32),
    )
    held = pl.pallas_call(
        functools.partial(kernel, patch_count, map_count, copies, scale),
        out_shape=results,
        in_specs=[hbm, hbm, hbm, hbm, hbm],
        out_specs=(vmem, vmem, vmem),
        scratch_shapes=[
            pltpu.SMEM((slots, nb), jnp.int32),
            pltpu.VMEM((order, chan, chan), BF16),
            pltpu.VMEM((nb, slots, bs, bs), BF16),
            pltpu.VMEM((nb, slots, bs, bs), BF16),
            field,
            field,
            own,
            own,
            wide,
            wide,
            rim,
            rim,
            rim,
            rim,
            pltpu.VMEM((patch_count, chan // 2, 2 * rows), F32),
            pltpu.VMEM((map_count, chan // 2, 2 * rows), F32),
            pltpu.VMEM((patch_count, chan // 4, 2 * rows), F32),
            pltpu.VMEM((map_count, chan // 4, 2 * rows), F32),
            pltpu.VMEM((rows, 4 * rows), BF16),
            pltpu.VMEM((rows, 4 * rows), BF16),
            dma,
            dma,
            dma((nb,)),
            dma((nb,)),
            dma((nb,)),
            dma((2, 2, REACH)),
            dma((2, 2, REACH)),
            dma((2, 2)),
            dma((2, 2)),
            dma((2, patch_count - 1)),
            dma((2, patch_count - 1)),
            dma((2, map_count - 1)),
            dma((2, map_count - 1)),
        ],
        compiler_params=pltpu.CompilerParams(
            collective_id=0, has_side_effects=True, vmem_limit_bytes=40 * 1024 * 1024
        ),
    )(
        pin(maps.reshape(rows, pix)), pin(cotangent.reshape(rows, pix)), pin(tiles), pin(columns.T), pin(filters)
    )
    out, grad, filter_grad = pl.pallas_call(
        write,
        out_shape=results,
        in_specs=[vmem] * 3,
        out_specs=(hbm,) * 3,
        scratch_shapes=[dma((3,))],
        compiler_params=pltpu.CompilerParams(vmem_limit_bytes=4 * 1024 * 1024),
    )(*held)
    return out.reshape(copies, chan, pix), grad.reshape(copies, chan, pix), filter_grad


def solution(mesh):
    field = P("map", None, "patch")
    return jax.shard_map(
        functools.partial(per_device, mesh.shape["patch"], mesh.shape["map"]),
        mesh=mesh,
        in_specs=(field, field, P("patch", None, None, None), P("patch", None), P()),
        out_specs=(field, field, P()),
        check_vma=False,
    )
```

profile of v0, /device:TPU:0, one launch (start us, length us, event | category | flops | bytes accessed | tf_op | source)
XLA Modules:
  0.0 20.0 jit_solution(5089612850989176039)
XLA Ops:
  0.6 18.6 %shard_map.76 = (bf16[64,1536]{1,0:T(8,128)(2,1)S(1)}, bf16[64,1536]{1,0:T(8,128)(2,1)S(1)}, f32[3,32,32]{2,1,0:T(8,128)S(1)}) custom-call(bf16[64,1536]{1,0:T(8,128)(2,1)} %bitcast.5, bf16[64,1536]{1,0:T(8,128)(2,1)} %bitcast.6, bf16[6,3,256,256]{3,2,1,0:T(8,128)(2,1)} %tiles_hbm.1, s32[3,6]{1,0:T(4,128)} %bitcast.7, bf16[3,32,32]{2,1,0:T(8,128)(2,1)} %filters_hbm.1), custom_call_target="tpu_custom_call" | custom-call | tf_op jit(solution)/shard_map/pallas_call | solution.py:445
  19.2 0.8 %shard_map.77 = (bf16[64,1536]{1,0:T(8,128)(2,1)}, bf16[64,1536]{1,0:T(8,128)(2,1)}, f32[3,32,32]{2,1,0:T(8,128)}) custom-call(bf16[64,1536]{1,0:T(8,128)(2,1)S(1)} %get-tuple-element.9.out, bf16[64,1536]{1,0:T(8,128)(2,1)S(1)} %get-tuple-element.10.grad, f32[3,32,32]{2,1,0:T(8,128)S(1)} %get-tuple-element.11.filter_grad), custom_call_target="tpu_custom_call" | custom-call | tf_op jit(solution)/shard_map/pallas_call | solution.py:491
where the time goes:
time: 20.1 us; the launch traced here: 20 us
  Pallas kernels  19.3 us (96%)
  between operations  0.64 us (3%)
    pallas_call x1, Pallas kernels, per_device(): pl.pallas_call(functools.partial(kernel, patch_count, map_count, copies,...  18.6 us
    pallas_call x1, Pallas kernels, per_device(): pl.pallas_call(write, out_shape=results, in_specs=[vmem] * 3, out_specs=(...  0.78 us

commit v1 on v0

--- a/solution.py
+++ b/solution.py
@@ -328,8 +328,6 @@
         loads_y[b].wait()
         loads_t[b].wait()
     adj, p1, p2 = send_adjoint(0, y_zero)
-    load_f.wait()
-    mix_in[...], mix_out[...] = mixing(filters, copies)
     for b in middle:
         loads_y[b].wait()
         loads_t[b].wait()
@@ -337,13 +335,14 @@
         loads_x[b].wait()
     for b in edges:
         acc_x[b] = inner_forward(x_zero, b)
-    for b in middle:
-        x_one[reach + b] = inner_forward(x_zero, b).astype(BF16)
+    local_adjoint(y_zero, p1, p2)
     for copy in halo:
         copy.wait_recv()
     for b in edges:
         x_one[reach + b] = (acc_x[b] + rest_forward(x_zero, b)).astype(BF16)
     halo = send_x_one()
+    for b in middle:
+        x_one[reach + b] = inner_forward(x_zero, b).astype(BF16)
 
     product = None
     for b in range(nb):
@@ -354,7 +353,6 @@
     mid = chan // 2
     early = start_patch(0, early_patch, lanes([zeroth[:mid], zeroth[mid:], first_order[:mid], first_order[mid:]]))
 
-    local_adjoint(y_zero, p1, p2)
     for copy in adj:
         copy.wait_recv()
     product = None
@@ -385,6 +383,8 @@
         terms = jnp.concatenate([first, y_one[b], coarse, fine], axis=0)
         grad[:, b * bs : (b + 1) * bs] = dot_nn(mix_in[...], terms).astype(BF16)
 
+    load_f.wait()
+    mix_in[...], mix_out[...] = mixing(filters, copies)
     late = start_map(1, late_map, total_of(late_patch, patch_count, late))
     local_adjoint(y_one, p1, p2)
     for b in middle:

time: 20.1 us -> 20.1 us (level)
  no operation moved by 1% of the time
where the time goes in v1:
time: 20.1 us; the launch traced here: 20 us
  Pallas kernels  19.3 us (96%)
  between operations  0.64 us (3%)
    pallas_call x1, Pallas kernels, per_device(): pl.pallas_call(functools.partial(kernel, patch_count, map_count, copies,...  18.6 us
    pallas_call x1, Pallas kernels, per_device(): pl.pallas_call(write, out_shape=results, in_specs=[vmem] * 3, out_specs=(...  0.78 us

profile of v1, /device:TPU:0, one launch (start us, length us, event | category | flops | bytes accessed | tf_op | source)
XLA Modules:
  0.0 20.0 jit_solution(10327815955002531463)
XLA Ops:
  0.6 18.6 %shard_map.76 = (bf16[64,1536]{1,0:T(8,128)(2,1)S(1)}, bf16[64,1536]{1,0:T(8,128)(2,1)S(1)}, f32[3,32,32]{2,1,0:T(8,128)S(1)}) custom-call(bf16[64,1536]{1,0:T(8,128)(2,1)} %bitcast.5, bf16[64,1536]{1,0:T(8,128)(2,1)} %bitcast.6, bf16[6,3,256,256]{3,2,1,0:T(8,128)(2,1)} %tiles_hbm.1, s32[3,6]{1,0:T(4,128)} %bitcast.7, bf16[3,32,32]{2,1,0:T(8,128)(2,1)} %filters_hbm.1), custom_call_target="tpu_custom_call" | custom-call | tf_op jit(solution)/shard_map/pallas_call | solution.py:445
  19.2 0.8 %shard_map.77 = (bf16[64,1536]{1,0:T(8,128)(2,1)}, bf16[64,1536]{1,0:T(8,128)(2,1)}, f32[3,32,32]{2,1,0:T(8,128)}) custom-call(bf16[64,1536]{1,0:T(8,128)(2,1)S(1)} %get-tuple-element.9.out, bf16[64,1536]{1,0:T(8,128)(2,1)S(1)} %get-tuple-element.10.grad, f32[3,32,32]{2,1,0:T(8,128)S(1)} %get-tuple-element.11.filter_grad), custom_call_target="tpu_custom_call" | custom-call | tf_op jit(solution)/shard_map/pallas_call | solution.py:491

commit v2 on v1

--- a/solution.py
+++ b/solution.py
@@ -106,6 +106,8 @@
     loads_y = [pltpu.make_async_copy(cot.at[:, pl.ds(b * bs, bs)], y_zero.at[b], load_y.at[b]) for b in range(nb)]
     loads_x = [pltpu.make_async_copy(maps.at[:, pl.ds(b * bs, bs)], x_zero.at[reach + b], load_x.at[b]) for b in range(nb)]
     loads_t = [pltpu.make_async_copy(tiles_hbm.at[b], tiles.at[b], load_tile.at[b]) for b in range(nb)]
+    for b in order:
+        loads_x[b].start()
     load_f = pltpu.make_async_copy(filters_hbm, filters, load_filters)
     load_f.start()
     load_c = pltpu.make_async_copy(cols_hbm, cols, load_cols)
@@ -113,9 +115,6 @@
     for b in order:
         loads_y[b].start()
         loads_t[b].start()
-    for b in order:
-        loads_x[b].start()
-
     def remote(src, dst, send_sem, recv_sem, patch, map_index):
         copy = pltpu.make_async_remote_copy(
             src_ref=src,
@@ -130,47 +129,21 @@
 
     sent = []
 
-    def send_maps():
-        copies_ = []
-        for i in range(reach):
-            copies_.append(
-                remote(
-                    maps.at[:, pl.ds(i * bs, bs)],
-                    x_zero.at[reach + nb + i],
-                    halo_send.at[0, 0, i],
-                    halo_recv.at[0, 0, i],
-                    left,
-                    my_map,
-                )
-            )
-            copies_.append(
-                remote(
-                    maps.at[:, pl.ds((nb - reach + i) * bs, bs)],
-                    x_zero.at[i],
-                    halo_send.at[0, 1, i],
-                    halo_recv.at[0, 1, i],
-                    right,
-                    my_map,
-                )
-            )
-        sent.extend(copies_)
-        return copies_
-
-    def send_x_one():
+    def send_halo(turn, field):
         copies_ = [
             remote(
-                x_one.at[pl.ds(reach, reach)],
-                x_one.at[pl.ds(reach + nb, reach)],
-                halo_send.at[1, 0, 0],
-                halo_recv.at[1, 0, 0],
+                field.at[pl.ds(reach, reach)],
+                field.at[pl.ds(reach + nb, reach)],
+                halo_send.at[turn, 0],
+                halo_recv.at[turn, 0],
                 left,
                 my_map,
             ),
             remote(
-                x_one.at[pl.ds(nb, reach)],
-                x_one.at[pl.ds(0, reach)],
-                halo_send.at[1, 1, 0],
-                halo_recv.at[1, 1, 0],
+                field.at[pl.ds(nb, reach)],
+                field.at[pl.ds(0, reach)],
+                halo_send.at[turn, 1],
+                halo_recv.at[turn, 1],
                 right,
                 my_map,
             ),
@@ -320,7 +293,9 @@
         return left_term(field, b) if b < reach else right_term(field, b)
 
     pl.semaphore_wait(barrier, patch_count + map_count - 2)
-    halo = send_maps()
+    for b in edges:
+        loads_x[b].wait()
+    halo = send_halo(0, x_zero)
     load_c.wait()
     near_left = [lax.rem(me * nb + b - cols[1, b] + total, total) == 1 for b in range(nb)]
     near_right = [lax.rem(cols[2, b] - me * nb - b + total, total) == 1 for b in range(nb)]
@@ -331,7 +306,7 @@
     for b in middle:
         loads_y[b].wait()
         loads_t[b].wait()
-    for b in range(nb):
+    for b in middle:
         loads_x[b].wait()
     for b in edges:
         acc_x[b] = inner_forward(x_zero, b)
@@ -340,7 +315,7 @@
         copy.wait_recv()
     for b in edges:
         x_one[reach + b] = (acc_x[b] + rest_forward(x_zero, b)).astype(BF16)
-    halo = send_x_one()
+    halo = send_halo(1, x_one)
     for b in middle:
         x_one[reach + b] = inner_forward(x_zero, b).astype(BF16)
 
@@ -473,8 +448,8 @@
             dma((nb,)),
             dma((nb,)),
             dma((nb,)),
-            dma((2, 2, REACH)),
-            dma((2, 2, REACH)),
+            dma((2, 2)),
+            dma((2, 2)),
             dma((2, 2)),
             dma((2, 2)),
             dma((2, patch_count - 1)),

time: 20.1 us -> 19.8 us (0.985)
    pallas_call x1, Pallas kernels: 18.6 us -> 18.3 us  [per_device(): pl.pallas_call(functools.partial(kernel, patch_count, map_count, copies,...]
where the time goes in v2:
time: 19.8 us; the launch traced here: 19.7 us
  Pallas kernels  19.1 us (96%)
  between operations  0.64 us (3%)
    pallas_call x1, Pallas kernels, per_device(): pl.pallas_call(functools.partial(kernel, patch_count, map_count, copies,...  18.3 us
    pallas_call x1, Pallas kernels, per_device(): pl.pallas_call(write, out_shape=results, in_specs=[vmem] * 3, out_specs=(...  0.78 us

profile of v2, /device:TPU:0, one launch (start us, length us, event | category | flops | bytes accessed | tf_op | source)
XLA Modules:
  0.0 19.7 jit_solution(11547380563055791169)
XLA Ops:
  0.6 18.3 %shard_map.76 = (bf16[64,1536]{1,0:T(8,128)(2,1)S(1)}, bf16[64,1536]{1,0:T(8,128)(2,1)S(1)}, f32[3,32,32]{2,1,0:T(8,128)S(1)}) custom-call(bf16[64,1536]{1,0:T(8,128)(2,1)} %bitcast.5, bf16[64,1536]{1,0:T(8,128)(2,1)} %bitcast.6, bf16[6,3,256,256]{3,2,1,0:T(8,128)(2,1)} %tiles_hbm.1, s32[3,6]{1,0:T(4,128)} %bitcast.7, bf16[3,32,32]{2,1,0:T(8,128)(2,1)} %filters_hbm.1), custom_call_target="tpu_custom_call" | custom-call | tf_op jit(solution)/shard_map/pallas_call | solution.py:420
  18.9 0.8 %shard_map.77 = (bf16[64,1536]{1,0:T(8,128)(2,1)}, bf16[64,1536]{1,0:T(8,128)(2,1)}, f32[3,32,32]{2,1,0:T(8,128)}) custom-call(bf16[64,1536]{1,0:T(8,128)(2,1)S(1)} %get-tuple-element.9.out, bf16[64,1536]{1,0:T(8,128)(2,1)S(1)} %get-tuple-element.10.grad, f32[3,32,32]{2,1,0:T(8,128)S(1)} %get-tuple-element.11.filter_grad), custom_call_target="tpu_custom_call" | custom-call | tf_op jit(solution)/shard_map/pallas_call | solution.py:466

commit v3 on v2

--- a/solution.py
+++ b/solution.py
@@ -369,14 +369,14 @@
         copy.wait_recv()
     for b in edges:
         write_output(b, acc_x[b] + rest_forward(x_one, b))
-    for copy in adj:
-        copy.wait_recv()
-    for b in edges:
-        write_grad(b)
     whole = total_of(early_map, map_count, early) * scale
     shifted = [pltpu.roll(whole, width - i * chan, 1)[:, :chan] if i else whole[:, :chan] for i in range(4)]
     filter_grad[0, :mid], filter_grad[0, mid:] = shifted[0], shifted[1]
     filter_grad[1, :mid], filter_grad[1, mid:] = shifted[2], shifted[3]
+    for copy in adj:
+        copy.wait_recv()
+    for b in edges:
+        write_grad(b)
     whole = total_of(late_map, map_count, late) * scale
     for i in range(4):
         lines = slice(i * quarter, (i + 1) * quarter)

time: 19.8 us -> 19.8 us (level)
  no operation moved by 1% of the time
where the time goes in v3:
time: 19.8 us; the launch traced here: 19.7 us
  Pallas kernels  19.1 us (96%)
  between operations  0.64 us (3%)
    pallas_call x1, Pallas kernels, per_device(): pl.pallas_call(functools.partial(kernel, patch_count, map_count, copies,...  18.3 us
    pallas_call x1, Pallas kernels, per_device(): pl.pallas_call(write, out_shape=results, in_specs=[vmem] * 3, out_specs=(...  0.78 us

profile of v3, /device:TPU:0, one launch (start us, length us, event | category | flops | bytes accessed | tf_op | source)
XLA Modules:
  0.0 19.7 jit_solution(4371193592977920918)
XLA Ops:
  0.6 18.3 %shard_map.76 = (bf16[64,1536]{1,0:T(8,128)(2,1)S(1)}, bf16[64,1536]{1,0:T(8,128)(2,1)S(1)}, f32[3,32,32]{2,1,0:T(8,128)S(1)}) custom-call(bf16[64,1536]{1,0:T(8,128)(2,1)} %bitcast.5, bf16[64,1536]{1,0:T(8,128)(2,1)} %bitcast.6, bf16[6,3,256,256]{3,2,1,0:T(8,128)(2,1)} %tiles_hbm.1, s32[3,6]{1,0:T(4,128)} %bitcast.7, bf16[3,32,32]{2,1,0:T(8,128)(2,1)} %filters_hbm.1), custom_call_target="tpu_custom_call" | custom-call | tf_op jit(solution)/shard_map/pallas_call | solution.py:420
  18.9 0.8 %shard_map.77 = (bf16[64,1536]{1,0:T(8,128)(2,1)}, bf16[64,1536]{1,0:T(8,128)(2,1)}, f32[3,32,32]{2,1,0:T(8,128)}) custom-call(bf16[64,1536]{1,0:T(8,128)(2,1)S(1)} %get-tuple-element.9.out, bf16[64,1536]{1,0:T(8,128)(2,1)S(1)} %get-tuple-element.10.grad, f32[3,32,32]{2,1,0:T(8,128)S(1)} %get-tuple-element.11.filter_grad), custom_call_target="tpu_custom_call" | custom-call | tf_op jit(solution)/shard_map/pallas_call | solution.py:466
